TPU v7x, 128 devices: a whole 4x4x4 slice. The times are simulated.
128 devices in a mesh: expert: 64 (over z, y, x), edata: 2 (over core).
Axes of the slice: x: 4, y: 4, z: 4, core: 2. Of those that a mesh axis runs over, the one named last changes fastest.
Arguments:
- tokens: bfloat16 [16384, 2048], P(('expert', 'edata')), may hold values from -6 to 6
- cotangent: bfloat16 [16384, 2048], P(('expert', 'edata')), may hold values from -4 to 4
- expert_ids: int32 [16384, 8], P(('expert', 'edata')), may hold values from 0 to 63, all different within a row; in each aligned block of 128 rows (0 to 127, 128 to 255, ...) at most 24 rows name the same one
- gates: float32 [16384, 8], P(('expert', 'edata')), may hold values from 0.05 to 0.5
- w_gate: bfloat16 [64, 2048, 384], P('expert'), may hold values from -0.125 to 0.125
- w_up: bfloat16 [64, 2048, 384], P('expert'), may hold values from -0.125 to 0.125
- w_down: bfloat16 [64, 384, 2048], P('expert'), may hold values from -0.3125 to 0.3125
Outputs:
- mixed: bfloat16 [16384, 2048], P(('expert', 'edata'))
- input_grad: bfloat16 [16384, 2048], P(('expert', 'edata'))
- grad_gate: float32 [64, 2048, 384], P('expert', 'edata')
- grad_up: float32 [64, 2048, 384], P('expert', 'edata')
- grad_down: float32 [64, 384, 2048], P('expert', None, 'edata')
Inputs may be any that keep to these rules, and one draw needn't show every extreme that they name: `expert_ids`: each token names 8 different experts. Among the rows of one device no expert is named more than 24 times, and in every draw some device names some expert exactly 24 times.
All inputs are finite; a program needn't handle non-finite values.
Results may differ from a plain program's by a relative error of at most 0.0064.
Values may be sent and summed in bfloat16 or wider, within the bound.
No kernel may reach another device: no remote copies, remote signals or barrier semaphores. Data moves between devices by JAX's collectives and lax.ppermute only.
A program may use at most 128 MiB of HBM per device.

v0:
```python
import jax
import jax.numpy as jnp
from jax import lax
from jax.sharding import PartitionSpec as P


def slot_table(expert_ids, n_experts, capacity):
    flat_ids = expert_ids.reshape(-1)
    assignments = flat_ids.shape[0]
    onehot = (flat_ids[:, None] == jnp.arange(n_experts, dtype=jnp.int32)[None, :]).astype(
        jnp.int32
    )
    before = jnp.cumsum(onehot, axis=0) - onehot
    slot_index = jnp.sum(before * onehot, axis=1)
    target = flat_ids * capacity + slot_index
    owners = (
        jnp.full((n_experts * capacity,), -1, jnp.int32)
        .at[target]
        .set(jnp.arange(assignments, dtype=jnp.int32))
    )
    return (owners, target)


def expert_forward(input_rows, w_gate_one, w_up_one, w_down_one):
    gate_pre = jnp.dot(input_rows, w_gate_one, preferred_element_type=jnp.float32)
    up_pre = jnp.dot(input_rows, w_up_one, preferred_element_type=jnp.float32)
    hidden = (jax.nn.silu(gate_pre) * up_pre).astype(jnp.bfloat16)
    expert_out = jnp.dot(hidden, w_down_one, preferred_element_type=jnp.float32).astype(
        jnp.bfloat16
    )
    return (expert_out, gate_pre, up_pre, hidden)


def hidden_grads(cot_rows, gate_pre, up_pre, w_down_one):
    hidden_grad = lax.dot_general(
        cot_rows, w_down_one, (((1,), (1,)), ((), ())), preferred_element_type=jnp.float32
    )
    sigmoid_gate = jax.nn.sigmoid(gate_pre)
    gate_grad = (
        hidden_grad * up_pre * sigmoid_gate * (1.0 + gate_pre * (1.0 - sigmoid_gate))
    ).astype(jnp.bfloat16)
    up_grad = (hidden_grad * gate_pre * sigmoid_gate).astype(jnp.bfloat16)
    return (gate_grad, up_grad)


def row_grads(gate_grad, up_grad, w_gate_one, w_up_one):
    first = lax.dot_general(
        gate_grad, w_gate_one, (((1,), (1,)), ((), ())), preferred_element_type=jnp.float32
    )
    second = lax.dot_general(
        up_grad, w_up_one, (((1,), (1,)), ((), ())), preferred_element_type=jnp.float32
    )
    return (first + second).astype(jnp.bfloat16)


def local(tokens, cotangent, expert_ids, gates, w_gate, w_up, w_down):
    n_experts = lax.axis_size("expert")
    row_count, top_count = expert_ids.shape
    capacity = 3 * row_count * top_count // (2 * n_experts)
    feature_width = tokens.shape[1]
    owners, target = slot_table(expert_ids, n_experts, capacity)
    is_live = owners >= 0
    assign = jnp.where(is_live, owners, 0)
    token_index = assign // top_count
    input_send = jnp.where(is_live[:, None], tokens[token_index], jnp.zeros((), tokens.dtype))
    input_send = input_send.reshape(n_experts, capacity, feature_width)
    weight = jnp.where(is_live, gates.reshape(-1)[assign], 0.0)
    cot_send = (weight[:, None] * cotangent[token_index].astype(jnp.float32)).astype(jnp.bfloat16)
    cot_send = cot_send.reshape(n_experts, capacity, feature_width)
    w_gate_one = w_gate[0]
    w_up_one = w_up[0]
    w_down_one = w_down[0]
    input_recv = lax.all_to_all(input_send, "expert", split_axis=0, concat_axis=0, tiled=True)
    input_rows = input_recv.reshape(-1, feature_width)
    expert_out, gate_pre, up_pre, hidden = expert_forward(
        input_rows, w_gate_one, w_up_one, w_down_one
    )
    out_back = lax.all_to_all(
        expert_out.reshape(n_experts, capacity, feature_width),
        "expert",
        split_axis=0,
        concat_axis=0,
        tiled=True,
    )
    cot_recv = lax.all_to_all(cot_send, "expert", split_axis=0, concat_axis=0, tiled=True)
    cot_rows = cot_recv.reshape(-1, feature_width)
    grad_down = jnp.dot(hidden.T, cot_rows, preferred_element_type=jnp.float32)
    gate_grad, up_grad = hidden_grads(cot_rows, gate_pre, up_pre, w_down_one)
    row_grad = row_grads(gate_grad, up_grad, w_gate_one, w_up_one)
    grad_gate = jnp.dot(input_rows.T, gate_grad, preferred_element_type=jnp.float32)
    grad_up = jnp.dot(input_rows.T, up_grad, preferred_element_type=jnp.float32)
    gate_share, up_share, down_share = (
        lax.psum_scatter(grad_gate, "edata", scatter_dimension=0, tiled=True),
        lax.psum_scatter(grad_up, "edata", scatter_dimension=0, tiled=True),
        lax.psum_scatter(grad_down, "edata", scatter_dimension=1, tiled=True),
    )
    row_grad = row_grad.reshape(n_experts, capacity, feature_width)
    grad_back = lax.all_to_all(row_grad, "expert", split_axis=0, concat_axis=0, tiled=True)
    returned = out_back.reshape(-1, feature_width)[target].reshape(
        row_count, top_count, feature_width
    )
    mixed = jnp.sum(gates[:, :, None] * returned.astype(jnp.float32), axis=1).astype(jnp.bfloat16)
    grad_rows = grad_back.reshape(-1, feature_width)[target].reshape(
        row_count, top_count, feature_width
    )
    input_grad = jnp.sum(grad_rows.astype(jnp.float32), axis=1).astype(jnp.bfloat16)
    return (mixed, input_grad, gate_share[None], up_share[None], down_share[None])


def solution(mesh):
    placed = (
        P(("expert", "edata"), None),
        P(("expert", "edata"), None),
        P(("expert", "edata"), None),
        P(("expert", "edata"), None),
        P("expert", None, None),
        P("expert", None, None),
        P("expert", None, None),
    )
    return jax.shard_map(
        local,
        mesh=mesh,
        in_specs=placed,
        out_specs=(
            P(("expert", "edata"), None),
            P(("expert", "edata"), None),
            P("expert", "edata", None),
            P("expert", "edata", None),
            P("expert", None, "edata"),
        ),
        check_vma=False,
    )
```

profile of v0, /device:TPU:18, one launch (start us, length us, event | category | flops | bytes accessed | tf_op | source)
XLA Modules:
  0.0 476.2 jit_solution(223238896089040385)
XLA Ops:
  9.2 18.0 %reduce-window.6 = s32[64,8,128]{2,1,0:T(8,128)S(1)} reduce-window(s32[64,8,128]{2,1,0:T(8,128)S(1)} %fusion.15, s32[]{:T(128)} %constant.18.clone.1), window={size=1x1x128 pad=0_0x0_0x127_0}, to_apply=%region_0.0 | reduce-window | flops 8323072 | bytes 524292 | tf_op jit(solution)/shard_map/reduce-window
  32.4 7.1 %gather_fusion = bf16[1536,2048]{1,0:T(8,128)(2,1)} fusion(bf16[128,2048]{1,0:T(8,128)(2,1)S(1)} %copy-done.2, s32[2048]{0:T(1024)S(1)} %pad_clamp_fusion.1), kind=kCustom, calls=%fused_computation | custom fusion | bytes 12589056 | tf_op jit(solution)/shard_map/gather | solution.py:65
  39.4 5.9 %broadcast_select_fusion = bf16[64,24,2048]{2,1,0:T(8,128)(2,1)} fusion(bf16[64,24,2048]{2,1,0:T(8,128)(2,1)} %bitcast.69, pred[64,24]{1,0:T(8,128)(4,1)S(1)} %broadcast_in_dim.47), kind=kLoop, calls=%fused_computation.12 | loop fusion | flops 3145728 | bytes 12584448 | tf_op jit(solution)/shard_map/jit(_where)/select_n | solution.py:65
  45.4 11.6 %all-to-all-start = ((bf16[64,24,2048]{2,1,0:T(8,128)(2,1)}), bf16[64,24,2048]{2,1,0:T(8,128)(2,1)}, u32[]{:S(2)}, u32[]{:S(2)}) async-start(bf16[64,24,2048]{2,1,0:T(8,128)(2,1)} %broadcast_select_fusion), calls=%async_computation | async-start | bytes 12582912 | tf_op jit(solution)/shard_map/all_to_all | solution.py:73
  57.2 5.9 %gather_fusion.2 = f32[1536]{0:T(1024)S(1)} fusion(f32[1024]{0:T(1024)S(1)} %reshape.106, s32[2048]{0:T(1024)S(1)} %pad_clamp_fusion), kind=kCustom, calls=%fused_computation.2 | custom fusion | bytes 18432 | tf_op jit(solution)/shard_map/gather | solution.py:67
  63.1 7.1 %gather_fusion.3 = bf16[1536,2048]{1,0:T(8,128)(2,1)} fusion(bf16[128,2048]{1,0:T(8,128)(2,1)S(1)} %copy-done.3, s32[2048]{0:T(1024)S(1)} %pad_clamp_fusion.1), kind=kCustom, calls=%fused_computation.3 | custom fusion | bytes 12589056 | tf_op jit(solution)/shard_map/gather | solution.py:68
  70.2 6.5 %fusion = bf16[64,24,2048]{2,1,0:T(8,128)(2,1)} fusion(bf16[64,24,2048]{2,1,0:T(8,128)(2,1)} %bitcast.68, f32[64,24]{1,0:T(8,128)S(1)} %mul.71), kind=kLoop, calls=%fused_computation.7 | loop fusion | flops 9437184 | bytes 12589056 | tf_op jit(solution)/shard_map/convert_element_type | solution.py:68
  76.7 63.8 %all-to-all-done = bf16[64,24,2048]{2,1,0:T(8,128)(2,1)} async-done(((bf16[64,24,2048]{2,1,0:T(8,128)(2,1)}), bf16[64,24,2048]{2,1,0:T(8,128)(2,1)}, u32[]{:S(2)}, u32[]{:S(2)}) %all-to-all-start) | async-done | bytes 6291488 | tf_op jit(solution)/shard_map/all_to_all | solution.py:73
  140.5 9.9 %all-to-all-start.2 = ((bf16[64,24,2048]{2,1,0:T(8,128)(2,1)}), bf16[64,24,2048]{2,1,0:T(8,128)(2,1)}, u32[]{:S(2)}, u32[]{:S(2)}) async-start(bf16[64,24,2048]{2,1,0:T(8,128)(2,1)} %fusion), calls=%async_computation.2 | async-start | bytes 12582912 | tf_op jit(solution)/shard_map/all_to_all | solution.py:85
  150.7 7.8 %fusion.6 = f32[1536,384]{1,0:T(8,128)} fusion(bf16[1536,2048]{1,0:T(8,128)(2,1)} %bitcast.5, bf16[1,2048,384]{2,1,0:T(8,128)(2,1)S(1)} %copy-done.7), kind=kOutput, calls=%fused_computation.22 | convolution fusion | flops 2415919104 | bytes 10223616 | tf_op jit(solution)/shard_map/dot_general | solution.py:26
  158.5 7.6 %fusion.10 = f32[1536,384]{1,0:T(8,128)} fusion(bf16[1536,2048]{1,0:T(8,128)(2,1)} %bitcast.5, bf16[1,2048,384]{2,1,0:T(8,128)(2,1)S(1)} %copy-done.5), kind=kOutput, calls=%fused_computation.26 | convolution fusion | flops 2415919104 | bytes 10223616 | tf_op jit(solution)/shard_map/dot_general | solution.py:25
  166.1 69.5 %all-to-all-done.2 = bf16[64,24,2048]{2,1,0:T(8,128)(2,1)} async-done(((bf16[64,24,2048]{2,1,0:T(8,128)(2,1)}), bf16[64,24,2048]{2,1,0:T(8,128)(2,1)}, u32[]{:S(2)}, u32[]{:S(2)}) %all-to-all-start.2) | async-done | bytes 6291488 | tf_op jit(solution)/shard_map/all_to_all | solution.py:85
  235.6 10.0 %multiply_convert_fusion = (bf16[1536,384]{1,0:T(8,128)(2,1)}, bf16[1536,384]{1,0:T(8,128)(2,1)}, bf16[1536,384]{1,0:T(8,128)(2,1)S(1)}) fusion(f32[1536,384]{1,0:T(8,128)} %fusion.10, f32[1536,384]{1,0:T(8,128)} %fusion.6, bf16[1536,2048]{1,0:T(8,128)(2,1)} %bitcast.13, bf16[1,384,2048]{2,1,0:T(8,128)(2,1)S(1)} %copy-done), kind=kOutput, calls=%fused_computation.14 | convolution fusion | flops 2425356288 | bytes 16121856 | tf_op jit(solution)/shard_map/dot_general | solution.py:35
  245.6 7.2 %fusion.22 = f32[384,2048]{1,0:T(8,128)} fusion(bf16[1536,384]{1,0:T(8,128)(2,1)S(1)} %get-tuple-element.9, bf16[1536,2048]{1,0:T(8,128)(2,1)} %bitcast.13), kind=kOutput, calls=%fused_computation.56 | convolution fusion | flops 2415919104 | bytes 10616832 | tf_op jit(solution)/shard_map/dot_general | solution.py:87
  252.8 5.8 %convolution_convert_fusion = bf16[1536,2048]{1,0:T(8,128)(2,1)} fusion(bf16[1536,384]{1,0:T(8,128)(2,1)S(1)} %get-tuple-element.9, bf16[1,384,2048]{2,1,0:T(8,128)(2,1)S(1)} %copy-done), kind=kOutput, calls=%fused_computation.11 | convolution fusion | flops 2419064832 | bytes 9043968 | tf_op jit(solution)/shard_map/dot_general | solution.py:28
  258.6 8.5 %all-to-all-start.1 = ((bf16[64,24,2048]{2,1,0:T(8,128)(2,1)}), bf16[64,24,2048]{2,1,0:T(8,128)(2,1)}, u32[]{:S(2)}, u32[]{:S(2)}) async-start(bf16[64,24,2048]{2,1,0:T(8,128)(2,1)} %bitcast.70), calls=%async_computation.1 | async-start | bytes 12582912 | tf_op jit(solution)/shard_map/all_to_all | solution.py:78
  267.1 8.0 %fusion.20 = f32[2048,384]{1,0:T(8,128)} fusion(bf16[1536,2048]{1,0:T(8,128)(2,1)} %bitcast.5, bf16[1536,384]{1,0:T(8,128)(2,1)S(1)} %copy-done.10), kind=kOutput, calls=%fused_computation.54 | convolution fusion | flops 2415919104 | bytes 10616832 | tf_op jit(solution)/shard_map/dot_general | solution.py:90
  287.2 65.0 %all-to-all-done.1 = bf16[64,24,2048]{2,1,0:T(8,128)(2,1)} async-done(((bf16[64,24,2048]{2,1,0:T(8,128)(2,1)}), bf16[64,24,2048]{2,1,0:T(8,128)(2,1)}, u32[]{:S(2)}, u32[]{:S(2)}) %all-to-all-start.1) | async-done | bytes 6291488 | tf_op jit(solution)/shard_map/all_to_all | solution.py:78
  352.2 8.5 %all-to-all-start.3 = ((bf16[64,24,2048]{2,1,0:T(8,128)(2,1)}), bf16[64,24,2048]{2,1,0:T(8,128)(2,1)}, u32[]{:S(2)}, u32[]{:S(2)}) async-start(bf16[64,24,2048]{2,1,0:T(8,128)(2,1)} %bitcast.67), calls=%async_computation.3 | async-start | bytes 12582912 | tf_op jit(solution)/shard_map/all_to_all | solution.py:98
  360.9 7.9 %fusion.21 = f32[2048,384]{1,0:T(8,128)} fusion(bf16[1536,2048]{1,0:T(8,128)(2,1)} %bitcast.5, bf16[1536,384]{1,0:T(8,128)(2,1)S(1)} %copy-done.9), kind=kOutput, calls=%fused_computation.55 | convolution fusion | flops 2415919104 | bytes 10616832 | tf_op jit(solution)/shard_map/dot_general | solution.py:91
  368.8 12.4 %gather_fusion.1 = bf16[1024,2048]{1,0:T(8,128)(2,1)} fusion(bf16[1536,2048]{1,0:T(8,128)(2,1)} %bitcast.10, s32[1024]{0:T(1024)S(1)} %broadcast_clamp_fusion), kind=kCustom, calls=%fused_computation.1 | custom fusion | bytes 8392704 | tf_op jit(solution)/shard_map/gather | solution.py:99
  381.2 64.6 %all-to-all-done.3 = bf16[64,24,2048]{2,1,0:T(8,128)(2,1)} async-done(((bf16[64,24,2048]{2,1,0:T(8,128)(2,1)}), bf16[64,24,2048]{2,1,0:T(8,128)(2,1)}, u32[]{:S(2)}, u32[]{:S(2)}) %all-to-all-start.3) | async-done | bytes 6291488 | tf_op jit(solution)/shard_map/all_to_all | solution.py:98
  445.8 12.5 %gather_fusion.4 = bf16[1024,2048]{1,0:T(8,128)(2,1)} fusion(bf16[1536,2048]{1,0:T(8,128)(2,1)} %bitcast.15, s32[1024]{0:T(1024)S(1)} %broadcast_clamp_fusion), kind=kCustom, calls=%fused_computation.4 | custom fusion | bytes 8392704 | tf_op jit(solution)/shard_map/gather | solution.py:103
  458.3 6.0 %bitcast_reduce_fusion = bf16[128,2048]{1,0:T(8,128)(2,1)} fusion(bf16[1024,2048]{1,0:T(8,128)(2,1)} %gather_fusion.4), kind=kLoop, calls=%fused_computation.13 | loop fusion | flops 1835008 | bytes 4718592 | tf_op jit(solution)/shard_map/reduce_sum | solution.py:106
  (63 shorter events, 25.1 us)
Async XLA Ops:
  7.2 228.5 %copy-start = (bf16[1,384,2048]{2,1,0:T(8,128)(2,1)S(1)}, bf16[1,384,2048]{2,1,0:T(8,128)(2,1)}, u32[]{:S(2)}) copy-start(bf16[1,384,2048]{2,1,0:T(8,128)(2,1)} %param.13) | copy-start | bytes 4718596
  7.2 25.2 %copy-start.2 = (bf16[128,2048]{1,0:T(8,128)(2,1)S(1)}, bf16[128,2048]{1,0:T(8,128)(2,1)}, u32[]{:S(2)}) copy-start(bf16[128,2048]{1,0:T(8,128)(2,1)} %param.7) | copy-start | bytes 1572868
  45.4 11.6 %copy-start.11 = (f32[128,8]{0,1:T(8,128)S(1)}, f32[128,8]{0,1:T(8,128)}, u32[]{:S(2)}) copy-start(f32[128,8]{0,1:T(8,128)} %param.10) | copy-start | bytes 12292
  45.4 95.1 %all-to-all-start = ((bf16[64,24,2048]{2,1,0:T(8,128)(2,1)}), bf16[64,24,2048]{2,1,0:T(8,128)(2,1)}, u32[]{:S(2)}, u32[]{:S(2)}) async-start(bf16[64,24,2048]{2,1,0:T(8,128)(2,1)} %broadcast_select_fusion), calls=%async_computation | async-start | bytes 12582912 | tf_op jit(solution)/shard_map/all_to_all | solution.py:73
  57.2 6.0 %copy-start.3 = (bf16[128,2048]{1,0:T(8,128)(2,1)S(1)}, bf16[128,2048]{1,0:T(8,128)(2,1)}, u32[]{:S(2)}) copy-start(bf16[128,2048]{1,0:T(8,128)(2,1)} %param.8) | copy-start | bytes 1572868
  76.7 74.0 %copy-start.7 = (bf16[1,2048,384]{2,1,0:T(8,128)(2,1)S(1)}, bf16[1,2048,384]{2,1,0:T(8,128)(2,1)}, u32[]{:S(2)}) copy-start(bf16[1,2048,384]{2,1,0:T(8,128)(2,1)} %param.12) | copy-start | bytes 4718596
  140.5 95.1 %all-to-all-start.2 = ((bf16[64,24,2048]{2,1,0:T(8,128)(2,1)}), bf16[64,24,2048]{2,1,0:T(8,128)(2,1)}, u32[]{:S(2)}, u32[]{:S(2)}) async-start(bf16[64,24,2048]{2,1,0:T(8,128)(2,1)} %fusion), calls=%async_computation.2 | async-start | bytes 12582912 | tf_op jit(solution)/shard_map/all_to_all | solution.py:85
  150.5 319.0 %reduce-scatter.8.cloned.1.call-start = ((), (), s32[]{:S(2)}) async-start(), calls=%async_computation.9 | async-start | bytes 4718592 | tf_op jit(solution)/shard_map/reduce_scatter | solution.py:95
  150.7 7.8 %copy-start.5 = (bf16[1,2048,384]{2,1,0:T(8,128)(2,1)S(1)}, bf16[1,2048,384]{2,1,0:T(8,128)(2,1)}, u32[]{:S(2)}) copy-start(bf16[1,2048,384]{2,1,0:T(8,128)(2,1)} %param.11) | copy-start | bytes 4718596
  258.6 8.6 %copy-start.10 = (bf16[1536,384]{1,0:T(8,128)(2,1)S(1)}, bf16[1536,384]{1,0:T(8,128)(2,1)}, u32[]{:S(2)}) copy-start(bf16[1536,384]{1,0:T(8,128)(2,1)} %get-tuple-element.8) | copy-start | bytes 3538948
  258.6 93.6 %all-to-all-start.1 = ((bf16[64,24,2048]{2,1,0:T(8,128)(2,1)}), bf16[64,24,2048]{2,1,0:T(8,128)(2,1)}, u32[]{:S(2)}, u32[]{:S(2)}) async-start(bf16[64,24,2048]{2,1,0:T(8,128)(2,1)} %bitcast.70), calls=%async_computation.1 | async-start | bytes 12582912 | tf_op jit(solution)/shard_map/all_to_all | solution.py:78
  267.1 202.4 %reduce-scatter.4.cloned.1.call-start = ((), (), s32[]{:S(2)}) async-start(), calls=%async_computation.7 | async-start | bytes 4718592 | tf_op jit(solution)/shard_map/reduce_scatter | solution.py:93
  275.1 1.4 copy-start.6
  276.5 4.9 %copy-start.8 = (bf16[1,2048,384]{2,1,0:T(8,128)(2,1)S(1)}, bf16[1,2048,384]{2,1,0:T(8,128)(2,1)}, u32[]{:S(2)}) copy-start(bf16[1,2048,384]{2,1,0:T(8,128)(2,1)} %param.12) | copy-start | bytes 4718596
  276.5 5.0 %copy-start.9 = (bf16[1536,384]{1,0:T(8,128)(2,1)S(1)}, bf16[1536,384]{1,0:T(8,128)(2,1)}, u32[]{:S(2)}) copy-start(bf16[1536,384]{1,0:T(8,128)(2,1)} %get-tuple-element.7) | copy-start | bytes 3538948
  352.2 93.6 %all-to-all-start.3 = ((bf16[64,24,2048]{2,1,0:T(8,128)(2,1)}), bf16[64,24,2048]{2,1,0:T(8,128)(2,1)}, u32[]{:S(2)}, u32[]{:S(2)}) async-start(bf16[64,24,2048]{2,1,0:T(8,128)(2,1)} %bitcast.67), calls=%async_computation.3 | async-start | bytes 12582912 | tf_op jit(solution)/shard_map/all_to_all | solution.py:98
  360.7 108.8 %reduce-scatter.6.cloned.1.call-start = ((), (), s32[]{:S(2)}) async-start(), calls=%async_computation.8 | async-start | bytes 4718592 | tf_op jit(solution)/shard_map/reduce_scatter | solution.py:94
  458.3 6.0 %copy-start.4 = (bf16[1024,2048]{1,0:T(8,128)(2,1)S(1)}, bf16[1024,2048]{1,0:T(8,128)(2,1)}, u32[]{:S(2)}) copy-start(bf16[1024,2048]{1,0:T(8,128)(2,1)} %gather_fusion.1) | copy-start | bytes 12582916
  458.3 11.2 %copy-start.1 = (bf16[1,384,2048]{2,1,0:T(8,128)(2,1)S(1)}, bf16[1,384,2048]{2,1,0:T(8,128)(2,1)}, u32[]{:S(2)}) copy-start(bf16[1,384,2048]{2,1,0:T(8,128)(2,1)} %param.13) | copy-start | bytes 4718596
Sparse Core Ops, SparseCore 0:
  252.9 12.7 reduce-scatter.7
  275.3 14.8 reduce-scatter.3
  368.9 14.8 reduce-scatter.5
where the time goes:
time: 483 us; the launch traced here: 476 us
  waiting for transfers between devices  263 us (54%)
  matrix products  64.8 us (13%)
  local copies, waits for them, and re-layouts  52.5 us (11%)
  other arithmetic  42.7 us (9%)
  starting transfers between devices  38.9 us (8%)
  between operations  14.2 us (3%)
    all_to_all x1, waiting for transfers between devices, local(): lax.all_to_all(cot_send, 'expert', split_axis=0, concat_axis=0, tiled=True)  69.5 us
    all_to_all x1, waiting for transfers between devices, local(): lax.all_to_all(expert_out.reshape(n_experts, capacity, feature_width), 'e...  65 us
    all_to_all x1, waiting for transfers between devices, local(): lax.all_to_all(row_grad, 'expert', split_axis=0, concat_axis=0, tiled=True)  64.6 us
    all_to_all x1, waiting for transfers between devices, local(): lax.all_to_all(input_send, 'expert', split_axis=0, concat_axis=0, tiled=T...  63.8 us
    another operation x3, other arithmetic  18.2 us
    gather x1, local copies, waits for them, and re-layouts, local(): grad_back.reshape(-1, feature_width)[target]  12.5 us
    gather x1, local copies, waits for them, and re-layouts, local(): out_back.reshape(-1, feature_width)[target]  12.4 us
    all_to_all x1, starting transfers between devices, local(): lax.all_to_all(input_send, 'expert', split_axis=0, concat_axis=0, tiled=T...  11.6 us
  transfers between devices with their start and end apart: 7, of which 4 were waited for; matrix products, arithmetic and copies ran while one was open for 22% of the time, Pallas kernels for 0%

commit v1 on v0

v1 whole, which is shorter than its diff:
```python
import jax
import jax.numpy as jnp
from jax import lax
from jax.experimental import pallas as pl
from jax.experimental.pallas import tpu as pltpu
from jax.sharding import Mesh, PartitionSpec as P

RING = 4
DEVS = 16
PAIRS = 8
CAP = 24
SLOTS = RING * 2 * CAP
BLOCK = 144
VMEM = 60 << 20
F32, BF16 = jnp.float32, jnp.bfloat16


def shift(block, axis, by):
    return lax.ppermute(block, axis, [(i, (i + by) % RING) for i in range(RING)])


def after(value, *others):
    return lax.optimization_barrier((value,) + others)[0]


def near(block, axis):
    return (block, shift(block, axis, 1), shift(block, axis, -1), shift(block, axis, 2))


def together(*groups):
    flat = lax.optimization_barrier(tuple(x for group in groups for x in group))
    out, at = [], 0
    for group in groups:
        out.append(flat[at : at + len(group)])
        at += len(group)
    return out


def sends(parts, axis):
    own, below, above, far = parts
    return (own, shift(above, axis, 1), shift(below, axis, -1), shift(far, axis, 2))


def total(parts):
    out = parts[0].astype(F32)
    for part in parts[1:]:
        out = out + part.astype(F32)
    return out.astype(BF16)


def cut(parts):
    rows = parts[0].shape[0] // RING
    return [total([part[i * rows : (i + 1) * rows] for part in parts]) for i in range(RING)]


def far_sends(parts, axis):
    return (shift(parts[3], axis, 1), shift(parts[4], axis, -1))


def side_sends(parts, pair, axis):
    own, below, above = parts[:3]
    half = pair[0].shape[0]
    above = jnp.concatenate([total((above[:half], pair[0])), above[half:]], 0)
    below = jnp.concatenate([below[:half], total((below[half:], pair[1]))], 0)
    return (own, shift(above, axis, 1), shift(below, axis, -1))


def params():
    return pltpu.CompilerParams(vmem_limit_bytes=VMEM)


def cost(flops, nbytes):
    return pl.CostEstimate(flops=int(flops), bytes_accessed=int(nbytes), transcendentals=0)


def piece(refs, outer, inner, rows):
    return refs[outer * 2 + inner // 2], (inner % 2) * rows


def make_tables(base, refs, slot_ref, gate_ref):
    row = lax.broadcasted_iota(jnp.int32, (256, 256), 0)
    col = lax.broadcasted_iota(jnp.int32, (256, 256), 1)
    before = jnp.where((row < col) & ((row < 128) == (col < 128)), 1.0, 0.0).astype(BF16)
    lane = lax.broadcasted_iota(jnp.int32, (RING, 256), 1)
    index = lax.broadcasted_iota(jnp.int32, (RING, 256), 0)
    for p in range(PAIRS):
        both = []
        for h in range(2):
            ref, first = piece(refs, p // 2, (p % 2) * 2 + h, BLOCK)
            both.append(ref[first + 128 : first + BLOCK, :256].astype(F32))
        ids = jnp.concatenate([t[:8, :128] for t in both], 1).astype(jnp.int32)
        gates = jnp.concatenate([t[8:, :128] + t[:8, 128:] + t[8:, 128:] for t in both], 1)
        chosen, weight = [], []
        for j in range(RING):
            match = ids == base + j * DEVS
            chosen.append(jnp.sum(jnp.where(match, 1.0, 0.0), axis=0, keepdims=True))
            weight.append(jnp.sum(jnp.where(match, gates, 0.0), axis=0, keepdims=True))
        chosen = jnp.concatenate(chosen, 0)
        place = jnp.dot(chosen.astype(BF16), before, preferred_element_type=F32)
        slot = place.astype(jnp.int32) + jnp.where(lane < 128, 0, CAP) + index * (2 * CAP)
        slot_ref[p] = jnp.where(chosen > 0.5, slot, -1)
        gate_ref[p] = jnp.concatenate(weight, 0)


def spread(slot, values):
    row = lax.broadcasted_iota(jnp.int32, (SLOTS, 256), 0)
    total = jnp.zeros((SLOTS, 256), F32)
    for j in range(RING):
        value = 1.0 if values is None else values[j : j + 1, :]
        total = jnp.where(slot[j : j + 1, :] == row, value, total)
    return total


def put_rows(out_ref, p, rows):
    for j in range(RING):
        out_ref[j, p * 2 * CAP : (p + 1) * 2 * CAP, :] = rows[j * 2 * CAP : (j + 1) * 2 * CAP]


def whole(*shape):
    return pl.BlockSpec(shape, lambda i: (0,) * len(shape))


def first_then(*shape):
    return pl.BlockSpec((1,) + shape, lambda i: (jnp.maximum(i - 1, 0),) + (0,) * len(shape))


def then_last(*shape):
    return pl.BlockSpec(
        (1,) + shape, lambda i: (jnp.minimum(i, RING - 1),) + (0,) * len(shape)
    )


def forward_kernel(base_ref, *refs):
    pieces, w_ref = refs[:8], refs[8]
    rows_ref, slot_ref, gate_ref, hidden_ref, factor_ref, held = refs[9:]
    step = pl.program_id(0)

    @pl.when(step == 0)
    def _():
        make_tables(base_ref[0], pieces, slot_ref, gate_ref)
        for p in range(PAIRS):
            onehot = spread(slot_ref[p], None).astype(BF16)
            blocks = []
            for h in range(2):
                ref, first = piece(pieces, p // 2, (p % 2) * 2 + h, BLOCK)
                blocks.append(ref[first : first + 128, :])
            tokens = jnp.concatenate(blocks, 0)
            put_rows(held, p, jnp.dot(onehot, tokens, preferred_element_type=F32).astype(BF16))

    @pl.when(step > 0)
    def _():
        rows = held[step - 1]
        rows_ref[0] = rows
        pre = jnp.dot(rows, w_ref[0], preferred_element_type=F32)
        inner = pre.shape[1] // 2
        gate, up = pre[:, :inner], pre[:, inner:]
        sig = jax.nn.sigmoid(gate)
        silu = gate * sig
        hidden_ref[0] = (silu * up).astype(BF16)
        factor_ref[0, :, :inner] = up * sig * (1.0 + gate * (1.0 - sig))
        factor_ref[0, :, inner:] = silu


def forward(base, pieces, w_gu):
    width, two = w_gu.shape[1:]
    cap = DEVS * CAP
    table = (PAIRS, RING, 256)
    return pl.pallas_call(
        forward_kernel,
        grid=(RING + 1,),
        out_shape=(
            jax.ShapeDtypeStruct((RING, cap, width), BF16),
            jax.ShapeDtypeStruct(table, jnp.int32),
            jax.ShapeDtypeStruct(table, F32),
            jax.ShapeDtypeStruct((RING, cap, two // 2), BF16),
            jax.ShapeDtypeStruct((RING, cap, two), F32),
        ),
        in_specs=[pl.BlockSpec(memory_space=pltpu.SMEM)]
        + [whole(*p.shape) for p in pieces]
        + [first_then(width, two)],
        out_specs=(
            first_then(cap, width),
            whole(*table),
            whole(*table),
            first_then(cap, two // 2),
            first_then(cap, two),
        ),
        scratch_shapes=[pltpu.VMEM((RING, cap, width), BF16)],
        name="forward",
        compiler_params=params(),
        cost_estimate=cost(11e9, 40e6),
    )(base, *pieces, w_gu)


def cot_kernel(slot_ref, gate_ref, *refs):
    pieces, hidden_ref, rows_ref, down_ref, held = refs[:8], *refs[8:]
    step = pl.program_id(0)

    @pl.when(step == 0)
    def _():
        for p in range(PAIRS):
            slot = slot_ref[p]
            onehot = spread(slot, None).astype(BF16)
            weight = jnp.sum(spread(slot, gate_ref[p]), axis=1, keepdims=True)
            blocks = []
            for h in range(2):
                ref, first = piece(pieces, (p % 2) * 2 + h, p // 2, 128)
                blocks.append(ref[first : first + 128, :])
            cot = jnp.concatenate(blocks, 0)
            rows = jnp.dot(onehot, cot, preferred_element_type=F32)
            put_rows(held, p, (rows * weight).astype(BF16))

    @pl.when(step > 0)
    def _():
        rows = held[step - 1]
        rows_ref[0] = rows
        dims = (((0,), (0,)), ((), ()))
        out = lax.dot_general(hidden_ref[0], rows, dims, preferred_element_type=F32)
        out = out.astype(BF16)
        half = out.shape[1] // 2
        down_ref[0, 0] = out[:, :half]
        down_ref[0, 1] = out[:, half:]


def take_cot(slot, gate, pieces, hidden):
    width = pieces[0].shape[1]
    cap, inner = hidden.shape[1:]
    table = (PAIRS, RING, 256)
    return pl.pallas_call(
        cot_kernel,
        grid=(RING + 1,),
        out_shape=(
            jax.ShapeDtypeStruct((RING, cap, width), BF16),
            jax.ShapeDtypeStruct((RING, 2, inner, width // 2), BF16),
        ),
        in_specs=[whole(*table)] * 2
        + [whole(*p.shape) for p in pieces]
        + [first_then(cap, inner)],
        out_specs=(first_then(cap, width), first_then(2, inner, width // 2)),
        scratch_shapes=[pltpu.VMEM((RING, cap, width), BF16)],
        name="take_cot",
        compiler_params=params(),
        cost_estimate=cost(6e9, 22e6),
    )(slot, gate, *pieces, hidden)


def part_of(refs, outer, inner):
    if outer < 3:
        return refs[outer], inner * 128
    return refs[3 + inner // 2], (inner % 2) * 128


def parts_of(width):
    big, small = (RING * 128, width), (RING * 64, width)
    return ((big,) * 3 + (small,) * 2) * 2


def give_rows(weighted, slot_ref, gate_ref, held, refs):
    width = held.shape[2] // 2
    dims = (((0,), (0,)), ((), ()))
    for p in range(PAIRS):
        slot = slot_ref[p]
        rows = held[:, p * 2 * CAP : (p + 1) * 2 * CAP, :].reshape(SLOTS, 2 * width)
        if weighted:
            weight = spread(slot, gate_ref[p])
            high = weight.astype(BF16)
            low = (weight - high.astype(F32)).astype(BF16)
            out = lax.dot_general(high, rows, dims, preferred_element_type=F32)
            out = out + lax.dot_general(low, rows, dims, preferred_element_type=F32)
        else:
            onehot = spread(slot, None).astype(BF16)
            out = lax.dot_general(onehot, rows, dims, preferred_element_type=F32)
        out = out.astype(BF16)
        for h in range(2):
            y, x = p // 2, (p % 2) * 2 + h
            block = out[h * 128 : (h + 1) * 128]
            ref, first = part_of(refs[:5], y, x)
            ref[first : first + 128, :] = block[:, :width]
            ref, first = part_of(refs[5:], x, y)
            ref[first : first + 128, :] = block[:, width:]


def out_kernel(slot_ref, gate_ref, hidden_ref, w_ref, *refs):
    step = pl.program_id(0)
    held = refs[10]

    @pl.when(step < RING)
    def _():
        out = jnp.dot(hidden_ref[0], w_ref[0], preferred_element_type=F32)
        held[step] = out.astype(BF16)

    @pl.when(step == RING)
    def _():
        give_rows(True, slot_ref, gate_ref, held, refs[:10])


def give_out(slot, gate, hidden, w_down):
    cap, inner = hidden.shape[1:]
    width = w_down.shape[2]
    table = (PAIRS, RING, 256)
    parts = parts_of(width // 2)
    return pl.pallas_call(
        out_kernel,
        grid=(RING + 1,),
        out_shape=tuple(jax.ShapeDtypeStruct(part, BF16) for part in parts),
        in_specs=[whole(*table)] * 2 + [then_last(cap, inner), then_last(inner, width)],
        out_specs=tuple(whole(*part) for part in parts),
        scratch_shapes=[pltpu.VMEM((RING, cap, width), BF16)],
        name="give_out",
        compiler_params=params(),
        cost_estimate=cost(9e9, 20e6),
    )(slot, gate, hidden, w_down)


def back_kernel(slot_ref, gate_ref, cot_ref, w_down_ref, factor_ref, w_gu_ref, *refs):
    step = pl.program_id(0)
    grad_ref, held = refs[10], refs[11]
    dims = (((1,), (1,)), ((), ()))

    @pl.when(step < RING)
    def _():
        hidden_grad = lax.dot_general(
            cot_ref[0], w_down_ref[0], dims, preferred_element_type=F32
        )
        inner = hidden_grad.shape[1]
        gate_grad = (hidden_grad * factor_ref[0, :, :inner]).astype(BF16)
        up_grad = (hidden_grad * factor_ref[0, :, inner:]).astype(BF16)
        both = jnp.concatenate([gate_grad, up_grad], 1)
        grad_ref[0] = both
        row = lax.dot_general(both, w_gu_ref[0], dims, preferred_element_type=F32)
        held[step] = row.astype(BF16)

    @pl.when(step == RING)
    def _():
        give_rows(False, slot_ref, gate_ref, held, refs[:10])


def give_back(slot, gate, cot_rows, w_down, factor, w_gu):
    cap, width = cot_rows.shape[1:]
    inner = w_down.shape[1]
    table = (PAIRS, RING, 256)
    parts = parts_of(width // 2)
    out = pl.pallas_call(
        back_kernel,
        grid=(RING + 1,),
        out_shape=tuple(jax.ShapeDtypeStruct(part, BF16) for part in parts)
        + (jax.ShapeDtypeStruct((RING, cap, 2 * inner), BF16),),
        in_specs=[whole(*table)] * 2
        + [
            then_last(cap, width),
            then_last(inner, width),
            then_last(cap, 2 * inner),
            then_last(width, 2 * inner),
        ],
        out_specs=tuple(whole(*part) for part in parts) + (then_last(cap, 2 * inner),),
        scratch_shapes=[pltpu.VMEM((RING, cap, width), BF16)],
        name="give_back",
        compiler_params=params(),
        cost_estimate=cost(15e9, 45e6),
    )(slot, gate, cot_rows, w_down, factor, w_gu)
    return out[:10], out[10]


def per_expert(*shape):
    return pl.BlockSpec((1,) + shape, lambda e: (e,) + (0,) * len(shape))


def outer_up_kernel(rows_ref, grad_ref, out_ref):
    dims = (((0,), (0,)), ((), ()))
    total = lax.dot_general(rows_ref[0], grad_ref[0], dims, preferred_element_type=F32)
    out_ref[0] = total.astype(BF16)


def outer_up(rows, grad):
    count, cap, width = rows.shape
    two = grad.shape[2]
    return pl.pallas_call(
        outer_up_kernel,
        grid=(count,),
        out_shape=jax.ShapeDtypeStruct((count, width, two), BF16),
        in_specs=[per_expert(cap, width), per_expert(cap, two)],
        out_specs=per_expert(width, two),
        name="outer_up",
        compiler_params=params(),
        cost_estimate=cost(8e9, 22e6),
    )(rows, grad)


def local(tokens, cotangent, expert_ids, gates, w_gate, w_up, w_down):
    width, inner = w_gate.shape[1:]
    half = width // 2
    core = lax.axis_index("edata")
    gate_half = lax.dynamic_slice_in_dim(w_gate[0], core * half, half, 0)
    up_half = lax.dynamic_slice_in_dim(w_up[0], core * half, half, 0)
    down_half = lax.dynamic_slice_in_dim(w_down[0], core * (inner // 2), inner // 2, 0)
    w_gu = lax.all_gather(
        jnp.concatenate([gate_half, up_half], 1), ("z", "edata"), axis=0, tiled=True
    ).reshape(RING, width, 2 * inner)
    w_dn = lax.all_gather(down_half, ("z", "edata"), axis=0, tiled=True).reshape(
        RING, inner, width
    )

    hi = lax.reduce_precision(gates.T, 8, 7)
    mid = lax.reduce_precision(gates.T - hi, 8, 7)
    ids = expert_ids.T.astype(F32)
    left = jnp.concatenate([ids, hi], 0)
    right = jnp.concatenate([mid, gates.T - hi - mid], 0)
    table = jnp.concatenate([left, right], 1).astype(BF16)
    table = jnp.pad(table, ((0, 0), (0, width - table.shape[1])))
    own_t, own_c = jnp.concatenate([tokens, table], 0), cotangent
    below_t, below_c = shift(own_t, "x", 1), shift(own_c, "y", 1)
    above_t, above_c = shift(own_t, "x", -1), shift(own_c, "y", -1)
    (own_t, below_t, above_t), (own_c, below_c, above_c) = together(
        (own_t, below_t, above_t), (own_c, below_c, above_c)
    )
    low_t, low_c = jnp.concatenate([own_t, below_t], 0), jnp.concatenate([own_c, below_c], 0)
    first_t = (shift(low_t, "y", 1), shift(low_t, "y", -1))
    first_c = (shift(low_c, "x", 1), shift(low_c, "x", -1))
    over_t = shift(own_t, "x", 2)
    over_c = shift(after(own_c, over_t), "y", 2)
    first_t, first_c, (above_t, above_c, over_t, over_c) = together(
        first_t, first_c, (above_t, above_c, over_t, over_c)
    )
    high_t, high_c = jnp.concatenate([above_t, over_t], 0), jnp.concatenate([above_c, over_c], 0)
    second_t = (shift(high_t, "y", 1), shift(high_t, "y", -1))
    second_c = (shift(high_c, "x", 1), shift(high_c, "x", -1))
    third_t, third_c = shift(first_t[0], "y", 1), shift(first_c[0], "x", 1)
    fourth_t, fourth_c = shift(second_t[1], "y", -1), shift(second_c[1], "x", -1)
    tok = (low_t, high_t, first_t[0], second_t[0], first_t[1], second_t[1], third_t, fourth_t)
    cot = (low_c, high_c, first_c[0], second_c[0], first_c[1], second_c[1], third_c, fourth_c)

    base = lax.axis_index("y") * RING + lax.axis_index("x")
    rows, slot, gate, hidden, factor = forward(base.reshape(1).astype(jnp.int32), tok, w_gu)
    out = give_out(slot, gate, hidden, w_dn)
    out_1, out_2 = out[:5], out[5:]
    far_1, far_2 = far_sends(out_1, "y"), far_sends(out_2, "x")
    cot_rows, down = take_cot(after(slot, *out), gate, cot, hidden)
    far_1, far_2, (cot_rows, down) = together(far_1, far_2, (cot_rows, down))
    down = down.reshape(2 * RING * inner, half)
    down_sum = lax.psum_scatter(down, ("z", "edata"), scatter_dimension=0, tiled=True)

    side_1, side_2 = side_sends(out_1, far_1, "y"), side_sends(out_2, far_2, "x")
    gin, grad = give_back(slot, gate, cot_rows, w_dn, factor, w_gu)
    side_1, side_2, gin, (grad,) = together(side_1, side_2, gin, (grad,))

    gin_1, gin_2 = gin[:5], gin[5:]
    far_1, far_2 = far_sends(gin_1, "y"), far_sends(gin_2, "x")
    near_1, near_2 = sends(cut(side_1), "x"), sends(cut(side_2), "y")
    both = outer_up(rows, grad).reshape(RING * width, 2 * inner)
    both_sum = lax.psum_scatter(both, ("z", "edata"), scatter_dimension=0, tiled=True)
    near_1, near_2, far_1, far_2 = together(near_1, near_2, far_1, far_2)

    side_1, side_2 = side_sends(gin_1, far_1, "y"), side_sends(gin_2, far_2, "x")
    last_1, last_2 = sends(cut(side_1), "x"), sends(cut(side_2), "y")
    mixed = jnp.concatenate([total(near_1), total(near_2)], 1)
    input_grad = jnp.concatenate([total(last_1), total(last_2)], 1)

    both_sum = both_sum.astype(F32)
    return (
        mixed,
        input_grad,
        both_sum[None, :, :inner],
        both_sum[None, :, inner:],
        down_sum.astype(F32)[None],
    )


def solution(mesh):
    grid = Mesh(mesh.devices.reshape(RING, RING, RING, 2), ("z", "y", "x", "edata"))
    expert = ("z", "y", "x")
    rows = P(expert + ("edata",), None)
    weight = P(expert, None, None)
    return jax.shard_map(
        local,
        mesh=grid,
        in_specs=(rows, rows, rows, rows, weight, weight, weight),
        out_specs=(
            rows,
            rows,
            P(expert, "edata", None),
            P(expert, "edata", None),
            P(expert, None, "edata"),
        ),
        check_vma=False,
    )
```

time: 483 us -> 325 us (0.67)
  the two profiles are of different devices: /device:TPU:18 before, /device:TPU:96 now
where the time goes in v1:
time: 325 us; the launch traced here: 319 us
  waiting for transfers between devices  132 us (41%)
  Pallas kernels  76.8 us (24%)
  starting transfers between devices  64.6 us (20%)
  other arithmetic  16.4 us (5%)
  between operations  14.8 us (5%)
  local copies, waits for them, and re-layouts  14.7 us (5%)
    ppermute x46, waiting for transfers between devices, shift(): lax.ppermute(block, axis, [(i, (i + by) % RING) for i in range(RING)])  132 us
    ppermute x46, starting transfers between devices, shift(): lax.ppermute(block, axis, [(i, (i + by) % RING) for i in range(RING)])  64.4 us
    pallas_call x1, Pallas kernels, give_back(): pl.pallas_call(back_kernel, grid=(RING + 1,), out_shape=tuple((jax.ShapeD...  21.1 us
    pallas_call x1, Pallas kernels, forward(): pl.pallas_call(forward_kernel, grid=(RING + 1,), out_shape=(jax.ShapeDtyp...  16.7 us
    pallas_call x1, Pallas kernels, give_out(): pl.pallas_call(out_kernel, grid=(RING + 1,), out_shape=tuple((jax.ShapeDt...  14.3 us
    pallas_call x1, Pallas kernels, take_cot(): pl.pallas_call(cot_kernel, grid=(RING + 1,), out_shape=(jax.ShapeDtypeStr...  13 us
    pallas_call x1, Pallas kernels, outer_up(): pl.pallas_call(outer_up_kernel, grid=(count,), out_shape=jax.ShapeDtypeSt...  11.7 us
    unnamed x70, local copies, waits for them, and re-layouts  7.82 us
  transfers between devices with their start and end apart: 50, of which 16 were waited for; matrix products, arithmetic and copies ran while one was open for 6% of the time, Pallas kernels for 24%

profile of v1, /device:TPU:96, one launch (start us, length us, event | category | flops | bytes accessed | tf_op | source)
XLA Modules:
  0.0 319.2 jit_solution(16760326467751420126)
XLA Ops:
  18.0 11.1 %collective-permute-done.2 = bf16[128,2048]{1,0:T(8,128)(2,1)S(1)} collective-permute-done((bf16[128,2048]{1,0:T(8,128)(2,1)S(1)}, bf16[128,2048]{1,0:T(8,128)(2,1)S(1)}, u32[]{:S(2)}, u32[]{:S(2)}) %collective-permute-start.2) | collective-permute-done | bytes 524320 | tf_op jit(solution)/shard_map/ppermute | solution.py:19
  37.8 12.6 %collective-permute-done.8 = bf16[144,2048]{1,0:T(8,128)(2,1)S(1)} collective-permute-done((bf16[144,2048]{1,0:T(8,128)(2,1)S(1)}, bf16[144,2048]{1,0:T(8,128)(2,1)S(1)}, u32[]{:S(2)}, u32[]{:S(2)}) %collective-permute-start.8) | collective-permute-done | bytes 589856 | tf_op jit(solution)/shard_map/ppermute | solution.py:19
  52.1 17.6 %collective-permute-done.6.refs_2_ = bf16[256,2048]{1,0:T(8,128)(2,1)S(1)} collective-permute-done((bf16[256,2048]{1,0:T(8,128)(2,1)S(1)}, bf16[256,2048]{1,0:T(8,128)(2,1)S(1)}, u32[]{:S(2)}, u32[]{:S(2)}) %collective-permute-start.6) | collective-permute-done | bytes 1048608 | tf_op jit(solution)/shard_map/ppermute | solution.py:19
  74.2 25.2 %collective-permute-done.11.refs_5_ = bf16[288,2048]{1,0:T(8,128)(2,1)} collective-permute-done((bf16[288,2048]{1,0:T(8,128)(2,1)S(1)}, bf16[288,2048]{1,0:T(8,128)(2,1)}, u32[]{:S(2)}, u32[]{:S(2)}) %collective-permute-start.11) | collective-permute-done | bytes 1179680 | tf_op jit(solution)/shard_map/ppermute | solution.py:19
  104.9 22.4 %collective-permute-done.19.refs_5_ = bf16[256,2048]{1,0:T(8,128)(2,1)} collective-permute-done((bf16[256,2048]{1,0:T(8,128)(2,1)}, bf16[256,2048]{1,0:T(8,128)(2,1)}, u32[]{:S(2)}, u32[]{:S(2)}) %collective-permute-start.19) | collective-permute-done | bytes 1048608 | tf_op jit(solution)/shard_map/ppermute | solution.py:19
  127.5 3.6 %collective-permute-start.21 = (bf16[256,2048]{1,0:T(8,128)(2,1)}, bf16[256,2048]{1,0:T(8,128)(2,1)}, u32[]{:S(2)}, u32[]{:S(2)}) collective-permute-start(bf16[256,2048]{1,0:T(8,128)(2,1)} %collective-permute-done.19.refs_5_), channel_id=1, source_target_pairs={{0,6},{2,0},{4,2},{6,4},{1,7},{3,1},{5,3},{7,5},{8,14},{10,8},{12,... | collective-permute-start | bytes 3145736 | tf_op jit(solution)/shard_map/ppermute | solution.py:19
  131.1 16.7 %forward.1 = (bf16[4,384,2048]{2,1,0:T(8,128)(2,1)}, s32[8,4,256]{2,1,0:T(4,128)}, f32[8,4,256]{2,1,0:T(4,128)}, bf16[4,384,384]{2,1,0:T(8,128)(2,1)}, f32[4,384,768]{2,1,0:T(8,128)}) custom-call(s32[1]{0:T(128)} %bitcast.base_ref, bf16[288,2048]{1,0:T(8,128)(2,1)} %copy-done.22, bf16[288,2048]{1,0:T(8,128)(2,1)} %copy-done.21, ...), custom_call_target="tpu_custom_call" | custom-call | flops 11000000512 | bytes 40000000 | tf_op jit(solution)/shard_map/forward/pallas_call | solution.py:168
  147.8 14.3 %give_out.1 = (bf16[512,1024]{1,0:T(8,128)(2,1)}, bf16[512,1024]{1,0:T(8,128)(2,1)}, bf16[512,1024]{1,0:T(8,128)(2,1)}, bf16[256,1024]{1,0:T(8,128)(2,1)}, bf16[...) custom-call(s32[8,4,256]{2,1,0:T(4,128)} %get-tuple-element.108.slot, ...), custom_call_target="tpu_custom_call" | custom-call | flops 8999999488 | bytes 20000000 | tf_op jit(solution)/shard_map/give_out/pallas_call | solution.py:302
  162.1 3.2 %collective-permute-start.15 = (bf16[256,1024]{1,0:T(8,128)(2,1)}, bf16[256,1024]{1,0:T(8,128)(2,1)S(1)}, u32[]{:S(2)}, u32[]{:S(2)}) collective-permute-start(bf16[256,1024]{1,0:T(8,128)(2,1)} %get-tuple-element.101), channel_id=1, source_target_pairs={{0,24},{8,0},{16,8},{24,16},{1,25},{9,1},{17,9},{25,17},{2,26},{10... | collective-permute-start | bytes 1572872 | tf_op jit(solution)/shard_map/ppermute | solution.py:19
  165.3 3.4 %collective-permute-start.17 = (bf16[256,1024]{1,0:T(8,128)(2,1)}, bf16[256,1024]{1,0:T(8,128)(2,1)S(1)}, u32[]{:S(2)}, u32[]{:S(2)}) collective-permute-start(bf16[256,1024]{1,0:T(8,128)(2,1)} %get-tuple-element.103), channel_id=1, source_target_pairs={{0,6},{2,0},{4,2},{6,4},{1,7},{3,1},{5,3},{7,5},{8,14},{10,8},{12,... | collective-permute-start | bytes 1572872 | tf_op jit(solution)/shard_map/ppermute | solution.py:19
  168.7 13.0 %take_cot.1 = (bf16[4,384,2048]{2,1,0:T(8,128)(2,1)}, bf16[4,2,384,1024]{3,2,1,0:T(8,128)(2,1)}) custom-call(s32[8,4,256]{2,1,0:T(4,128)} %get-tuple-element.108.slot_ref, f32[8,4,256]{2,1,0:T(4,128)} %get-tuple-element.96.gate_ref, bf16[256,2048]{1,0:T(8,128)(2,1)} %copy-done.23, bf16[256,2048]{1,0:T(8,128)(2,1)} %constant_dynamic-update-slice_fusion.6.refs_1_, ...), custom_call_target="tpu_custom_call" | custom-call | flops 6000000000 | bytes 22000000 | tf_op jit(solution)/shard_map/take_cot/pallas_call | solution.py:229
  190.8 3.5 %collective-permute-start.25 = (bf16[512,1024]{1,0:T(8,128)(2,1)S(1)}, bf16[512,1024]{1,0:T(8,128)(2,1)}, u32[]{:S(2)}, u32[]{:S(2)}) collective-permute-start(bf16[512,1024]{1,0:T(8,128)(2,1)S(1)} %pad_maximum_fusion.4), channel_id=1, source_target_pairs={{0,6},{2,0},{4,2},{6,4},{1,7},{3,1},{5,3},{7,5},{8,14},{10,8},{12,... | collective-permute-start | bytes 3145736 | tf_op jit(solution)/shard_map/ppermute | solution.py:19
  194.3 21.1 %give_back.1 = (bf16[512,1024]{1,0:T(8,128)(2,1)}, bf16[512,1024]{1,0:T(8,128)(2,1)}, bf16[512,1024]{1,0:T(8,128)(2,1)}, bf16[256,1024]{1,0:T(8,128)(2,1)}, bf16...) custom-call(s32[8,4,256]{2,1,0:T(4,128)} %get-tuple-element.108.slot, ...), custom_call_target="tpu_custom_call" | custom-call | flops 15000000512 | bytes 45000000 | tf_op jit(solution)/shard_map/give_back/pallas_call | solution.py:343
  215.4 11.7 %outer_up.1 = bf16[4,2048,768]{2,1,0:T(8,128)(2,1)} custom-call(bf16[4,384,2048]{2,1,0:T(8,128)(2,1)} %get-tuple-element.160.rows_ref, bf16[4,384,768]{2,1,0:T(8,128)(2,1)} %get-tuple-element.161.grad_ref), custom_call_target="tpu_custom_call" | custom-call | flops 8000000000 | bytes 22000000 | tf_op jit(solution)/shard_map/outer_up/pallas_call | solution.py:377
  230.7 3.2 %collective-permute-start.27 = (bf16[128,1024]{1,0:T(8,128)(2,1)S(1)}, bf16[128,1024]{1,0:T(8,128)(2,1)S(1)}, u32[]{:S(2)}, u32[]{:S(2)}) collective-permute-start(bf16[128,1024]{1,0:T(8,128)(2,1)S(1)} %get-tuple-element.176), channel_id=1, source_target_pairs={{0,6},{2,0},{4,2},{6,4},{1,7},{3,1},{5,3},{7,5},{8,14},{10,8},{12,... | collective-permute-start | bytes 786440 | tf_op jit(solution)/shard_map/ppermute | solution.py:19
  243.9 3.8 %collective-permute-done.29 = bf16[128,1024]{1,0:T(8,128)(2,1)S(1)} collective-permute-done((bf16[128,1024]{1,0:T(8,128)(2,1)S(1)}, bf16[128,1024]{1,0:T(8,128)(2,1)S(1)}, u32[]{:S(2)}, u32[]{:S(2)}) %collective-permute-start.29) | collective-permute-done | bytes 262176 | tf_op jit(solution)/shard_map/ppermute | solution.py:19
  250.0 6.7 %collective-permute-done.31 = bf16[128,1024]{1,0:T(8,128)(2,1)S(1)} collective-permute-done((bf16[128,1024]{1,0:T(8,128)(2,1)S(1)}, bf16[128,1024]{1,0:T(8,128)(2,1)S(1)}, u32[]{:S(2)}, u32[]{:S(2)}) %collective-permute-start.31) | collective-permute-done | bytes 262176 | tf_op jit(solution)/shard_map/ppermute | solution.py:19
  257.5 3.2 collective-permute-done.35
  268.3 11.1 %collective-permute-done.42 = bf16[512,1024]{1,0:T(8,128)(2,1)S(1)} collective-permute-done((bf16[512,1024]{1,0:T(8,128)(2,1)S(1)}, bf16[512,1024]{1,0:T(8,128)(2,1)S(1)}, u32[]{:S(2)}, u32[]{:S(2)}) %collective-permute-start.42) | collective-permute-done | bytes 1048608 | tf_op jit(solution)/shard_map/ppermute | solution.py:19
  280.9 4.5 %collective-permute-start.44 = (bf16[128,1024]{1,0:T(8,128)(2,1)S(1)}, bf16[128,1024]{1,0:T(8,128)(2,1)S(1)}, u32[]{:S(2)}, u32[]{:S(2)}) collective-permute-start(bf16[128,1024]{1,0:T(8,128)(2,1)S(1)} %get-tuple-element.170), channel_id=1, source_target_pairs={{0,24},{8,0},{16,8},{24,16},{1,25},{9,1},{17,9},{25,17},{2,26},{10... | collective-permute-start | bytes 786440 | tf_op jit(solution)/shard_map/ppermute | solution.py:19
  286.1 3.7 %collective-permute-done.37 = bf16[512,1024]{1,0:T(8,128)(2,1)S(1)} collective-permute-done((bf16[512,1024]{1,0:T(8,128)(2,1)S(1)}, bf16[512,1024]{1,0:T(8,128)(2,1)S(1)}, u32[]{:S(2)}, u32[]{:S(2)}) %collective-permute-start.37) | collective-permute-done | bytes 1048608 | tf_op jit(solution)/shard_map/ppermute | solution.py:19
  289.9 3.8 %collective-permute-done.36 = bf16[512,1024]{1,0:T(8,128)(2,1)S(1)} collective-permute-done((bf16[512,1024]{1,0:T(8,128)(2,1)S(1)}, bf16[512,1024]{1,0:T(8,128)(2,1)S(1)}, u32[]{:S(2)}, u32[]{:S(2)}) %collective-permute-start.36) | collective-permute-done | bytes 1048608 | tf_op jit(solution)/shard_map/ppermute | solution.py:19
  298.2 3.8 %collective-permute-done.40 = bf16[128,1024]{1,0:T(8,128)(2,1)S(1)} collective-permute-done((bf16[128,1024]{1,0:T(8,128)(2,1)S(1)}, bf16[128,1024]{1,0:T(8,128)(2,1)S(1)}, u32[]{:S(2)}, u32[]{:S(2)}) %collective-permute-start.40) | collective-permute-done | bytes 262176 | tf_op jit(solution)/shard_map/ppermute | solution.py:19
  302.0 3.1 collective-permute-done.39
  (203 shorter events, 78.0 us)
Async XLA Ops:
  7.2 123.9 %all-gather.4.cloned.1.call-start = ((), (), s32[]{:S(2)}) async-start(), calls=%async_computation.2 | async-start | bytes 14155776 | tf_op jit(solution)/shard_map/all_gather | solution.py:396
  10.2 137.6 %all-gather.6.cloned.1.call-start = ((), (), s32[]{:S(2)}) async-start(), calls=%async_computation.5 | async-start | bytes 7077888 | tf_op jit(solution)/shard_map/all_gather | solution.py:399
  11.3 295.0 %reduce-scatter.5.cloned.1.call-start = ((), (), s32[]{:S(2)}) async-start(), calls=%async_computation.4 | async-start | bytes 7077888 | tf_op jit(solution)/shard_map/reduce_scatter | solution.py:440
  29.3 40.5 %collective-permute-start.4 = (bf16[288,2048]{1,0:T(8,128)(2,1)S(1)}, bf16[288,2048]{1,0:T(8,128)(2,1)}, u32[]{:S(2)}, u32[]{:S(2)}) collective-permute-start(bf16[288,2048]{1,0:T(8,128)(2,1)S(1)} %constant_dynamic-update-slice_fusion.refs_0_), channel_id=1, source_target_pairs={{0,8},{8,16},{16,24},{24,0},{1,9},{9,17},{17,25},{25,1},{2,10},{10... | collective-permute-start | bytes 3538952 | tf_op jit(solution)/shard_map/ppermute | solution.py:19
  30.9 40.2 %collective-permute-start.5 = (bf16[288,2048]{1,0:T(8,128)(2,1)S(1)}, bf16[288,2048]{1,0:T(8,128)(2,1)S(1)}, u32[]{:S(2)}, u32[]{:S(2)}) collective-permute-start(bf16[288,2048]{1,0:T(8,128)(2,1)S(1)} %constant_dynamic-update-slice_fusion.refs_0_), channel_id=1, source_target_pairs={{0,24},{8,0},{16,8},{24,16},{1,25},{9,1},{17,9},{25,17},{2,26},{10... | collective-permute-start | bytes 3538952 | tf_op jit(solution)/shard_map/ppermute | solution.py:19
  34.5 35.2 %collective-permute-start.6 = (bf16[256,2048]{1,0:T(8,128)(2,1)S(1)}, bf16[256,2048]{1,0:T(8,128)(2,1)S(1)}, u32[]{:S(2)}, u32[]{:S(2)}) collective-permute-start(bf16[256,2048]{1,0:T(8,128)(2,1)S(1)} %constant_dynamic-update-slice_fusion.2.refs_0_), channel_id=1, source_target_pairs={{0,2},{2,4},{4,6},{6,0},{1,3},{3,5},{5,7},{7,1},{8,10},{10,12},{12... | collective-permute-start | bytes 3145736 | tf_op jit(solution)/shard_map/ppermute | solution.py:19
  35.2 34.5 %collective-permute-start.7 = (bf16[256,2048]{1,0:T(8,128)(2,1)S(1)}, bf16[256,2048]{1,0:T(8,128)(2,1)S(1)}, u32[]{:S(2)}, u32[]{:S(2)}) collective-permute-start(bf16[256,2048]{1,0:T(8,128)(2,1)S(1)} %constant_dynamic-update-slice_fusion.2.refs_0_), channel_id=1, source_target_pairs={{0,6},{2,0},{4,2},{6,4},{1,7},{3,1},{5,3},{7,5},{8,14},{10,8},{12,... | collective-permute-start | bytes 3145736 | tf_op jit(solution)/shard_map/ppermute | solution.py:19
  71.2 28.2 %collective-permute-start.11 = (bf16[288,2048]{1,0:T(8,128)(2,1)S(1)}, bf16[288,2048]{1,0:T(8,128)(2,1)}, u32[]{:S(2)}, u32[]{:S(2)}) collective-permute-start(bf16[288,2048]{1,0:T(8,128)(2,1)S(1)} %constant_dynamic-update-slice_fusion.4.refs_1_), channel_id=1, source_target_pairs={{0,24},{8,0},{16,8},{24,16},{1,25},{9,1},{17,9},{25,17},{2,26},{10... | collective-permute-start | bytes 3538952 | tf_op jit(solution)/shard_map/ppermute | solution.py:19
  72.8 54.7 %collective-permute-start.10 = (bf16[288,2048]{1,0:T(8,128)(2,1)S(1)}, bf16[288,2048]{1,0:T(8,128)(2,1)}, u32[]{:S(2)}, u32[]{:S(2)}) collective-permute-start(bf16[288,2048]{1,0:T(8,128)(2,1)S(1)} %constant_dynamic-update-slice_fusion.4.refs_1_), channel_id=1, source_target_pairs={{0,8},{8,16},{16,24},{24,0},{1,9},{9,17},{17,25},{25,1},{2,10},{10... | collective-permute-start | bytes 3538952 | tf_op jit(solution)/shard_map/ppermute | solution.py:19
  73.3 57.7 %collective-permute-start.12 = (bf16[288,2048]{1,0:T(8,128)(2,1)}, bf16[288,2048]{1,0:T(8,128)(2,1)}, u32[]{:S(2)}, u32[]{:S(2)}) collective-permute-start(bf16[288,2048]{1,0:T(8,128)(2,1)} %collective-permute-done.4.refs_2_), channel_id=1, source_target_pairs={{0,8},{8,16},{16,24},{24,0},{1,9},{9,17},{17,25},{25,1},{2,10},{10... | collective-permute-start | bytes 3538952 | tf_op jit(solution)/shard_map/ppermute | solution.py:19
  99.4 31.6 %collective-permute-start.13 = (bf16[288,2048]{1,0:T(8,128)(2,1)}, bf16[288,2048]{1,0:T(8,128)(2,1)}, u32[]{:S(2)}, u32[]{:S(2)}) collective-permute-start(bf16[288,2048]{1,0:T(8,128)(2,1)} %collective-permute-done.11.refs_5_), channel_id=1, source_target_pairs={{0,24},{8,0},{16,8},{24,16},{1,25},{9,1},{17,9},{25,17},{2,26},{10... | collective-permute-start | bytes 3538952 | tf_op jit(solution)/shard_map/ppermute | solution.py:19
  102.9 24.4 %collective-permute-start.19 = (bf16[256,2048]{1,0:T(8,128)(2,1)}, bf16[256,2048]{1,0:T(8,128)(2,1)}, u32[]{:S(2)}, u32[]{:S(2)}) collective-permute-start(bf16[256,2048]{1,0:T(8,128)(2,1)} %constant_dynamic-update-slice_fusion.6.refs_1_), channel_id=1, source_target_pairs={{0,6},{2,0},{4,2},{6,4},{1,7},{3,1},{5,3},{7,5},{8,14},{10,8},{12,... | collective-permute-start | bytes 3145736 | tf_op jit(solution)/shard_map/ppermute | solution.py:19
  104.7 60.6 %collective-permute-start.18 = (bf16[256,2048]{1,0:T(8,128)(2,1)}, bf16[256,2048]{1,0:T(8,128)(2,1)}, u32[]{:S(2)}, u32[]{:S(2)}) collective-permute-start(bf16[256,2048]{1,0:T(8,128)(2,1)} %constant_dynamic-update-slice_fusion.6.refs_1_), channel_id=1, source_target_pairs={{0,2},{2,4},{4,6},{6,0},{1,3},{3,5},{5,7},{7,1},{8,10},{10,12},{12... | collective-permute-start | bytes 3145736 | tf_op jit(solution)/shard_map/ppermute | solution.py:19
  127.3 38.0 %collective-permute-start.20 = (bf16[256,2048]{1,0:T(8,128)(2,1)}, bf16[256,2048]{1,0:T(8,128)(2,1)}, u32[]{:S(2)}, u32[]{:S(2)}) collective-permute-start(bf16[256,2048]{1,0:T(8,128)(2,1)} %copy-done.27), channel_id=1, source_target_pairs={{0,2},{2,4},{4,6},{6,0},{1,3},{3,5},{5,7},{7,1},{8,10},{10,12},{12... | collective-permute-start | bytes 3145736 | tf_op jit(solution)/shard_map/ppermute | solution.py:19
  127.5 41.2 %collective-permute-start.21 = (bf16[256,2048]{1,0:T(8,128)(2,1)}, bf16[256,2048]{1,0:T(8,128)(2,1)}, u32[]{:S(2)}, u32[]{:S(2)}) collective-permute-start(bf16[256,2048]{1,0:T(8,128)(2,1)} %collective-permute-done.19.refs_5_), channel_id=1, source_target_pairs={{0,6},{2,0},{4,2},{6,4},{1,7},{3,1},{5,3},{7,5},{8,14},{10,8},{12,... | collective-permute-start | bytes 3145736 | tf_op jit(solution)/shard_map/ppermute | solution.py:19
  162.1 19.6 %collective-permute-start.14 = (bf16[256,1024]{1,0:T(8,128)(2,1)}, bf16[256,1024]{1,0:T(8,128)(2,1)S(1)}, u32[]{:S(2)}, u32[]{:S(2)}) collective-permute-start(bf16[256,1024]{1,0:T(8,128)(2,1)} %get-tuple-element.100), channel_id=1, source_target_pairs={{0,8},{8,16},{16,24},{24,0},{1,9},{9,17},{17,25},{25,1},{2,10},{10... | collective-permute-start | bytes 1572872 | tf_op jit(solution)/shard_map/ppermute | solution.py:19
  162.1 19.6 %collective-permute-start.15 = (bf16[256,1024]{1,0:T(8,128)(2,1)}, bf16[256,1024]{1,0:T(8,128)(2,1)S(1)}, u32[]{:S(2)}, u32[]{:S(2)}) collective-permute-start(bf16[256,1024]{1,0:T(8,128)(2,1)} %get-tuple-element.101), channel_id=1, source_target_pairs={{0,24},{8,0},{16,8},{24,16},{1,25},{9,1},{17,9},{25,17},{2,26},{10... | collective-permute-start | bytes 1572872 | tf_op jit(solution)/shard_map/ppermute | solution.py:19
  182.7 126.0 %reduce-scatter.3.cloned.1.call-start = ((), (), s32[]{:S(2)}) async-start(), calls=%async_computation.3 | async-start | bytes 14155776 | tf_op jit(solution)/shard_map/reduce_scatter | solution.py:450
  185.6 29.8 %collective-permute-start.22 = (bf16[512,1024]{1,0:T(8,128)(2,1)S(1)}, bf16[512,1024]{1,0:T(8,128)(2,1)}, u32[]{:S(2)}, u32[]{:S(2)}) collective-permute-start(bf16[512,1024]{1,0:T(8,128)(2,1)S(1)} %pad_maximum_fusion.1), channel_id=1, source_target_pairs={{0,8},{8,16},{16,24},{24,0},{1,9},{9,17},{17,25},{25,1},{2,10},{10... | collective-permute-start | bytes 3145736 | tf_op jit(solution)/shard_map/ppermute | solution.py:19
  186.8 28.6 %collective-permute-start.23 = (bf16[512,1024]{1,0:T(8,128)(2,1)S(1)}, bf16[512,1024]{1,0:T(8,128)(2,1)}, u32[]{:S(2)}, u32[]{:S(2)}) collective-permute-start(bf16[512,1024]{1,0:T(8,128)(2,1)S(1)} %pad_maximum_fusion.2), channel_id=1, source_target_pairs={{0,24},{8,0},{16,8},{24,16},{1,25},{9,1},{17,9},{25,17},{2,26},{10... | collective-permute-start | bytes 3145736 | tf_op jit(solution)/shard_map/ppermute | solution.py:19
  190.5 24.9 %collective-permute-start.24 = (bf16[512,1024]{1,0:T(8,128)(2,1)}, bf16[512,1024]{1,0:T(8,128)(2,1)}, u32[]{:S(2)}, u32[]{:S(2)}) collective-permute-start(bf16[512,1024]{1,0:T(8,128)(2,1)} %pad_maximum_fusion.3), channel_id=1, source_target_pairs={{0,2},{2,4},{4,6},{6,0},{1,3},{3,5},{5,7},{7,1},{8,10},{10,12},{12... | collective-permute-start | bytes 3145736 | tf_op jit(solution)/shard_map/ppermute | solution.py:19
  190.8 24.6 %collective-permute-start.25 = (bf16[512,1024]{1,0:T(8,128)(2,1)S(1)}, bf16[512,1024]{1,0:T(8,128)(2,1)}, u32[]{:S(2)}, u32[]{:S(2)}) collective-permute-start(bf16[512,1024]{1,0:T(8,128)(2,1)S(1)} %pad_maximum_fusion.4), channel_id=1, source_target_pairs={{0,6},{2,0},{4,2},{6,4},{1,7},{3,1},{5,3},{7,5},{8,14},{10,8},{12,... | collective-permute-start | bytes 3145736 | tf_op jit(solution)/shard_map/ppermute | solution.py:19
  264.6 25.2 %collective-permute-start.37 = (bf16[512,1024]{1,0:T(8,128)(2,1)S(1)}, bf16[512,1024]{1,0:T(8,128)(2,1)S(1)}, u32[]{:S(2)}, u32[]{:S(2)}) collective-permute-start(bf16[512,1024]{1,0:T(8,128)(2,1)S(1)} %pad_maximum_fusion.6), channel_id=1, source_target_pairs={{0,24},{8,0},{16,8},{24,16},{1,25},{9,1},{17,9},{25,17},{2,26},{10... | collective-permute-start | bytes 3145736 | tf_op jit(solution)/shard_map/ppermute | solution.py:19
  265.3 28.4 %collective-permute-start.36 = (bf16[512,1024]{1,0:T(8,128)(2,1)S(1)}, bf16[512,1024]{1,0:T(8,128)(2,1)S(1)}, u32[]{:S(2)}, u32[]{:S(2)}) collective-permute-start(bf16[512,1024]{1,0:T(8,128)(2,1)S(1)} %pad_maximum_fusion.5), channel_id=1, source_target_pairs={{0,8},{8,16},{16,24},{24,0},{1,9},{9,17},{17,25},{25,1},{2,10},{10... | collective-permute-start | bytes 3145736 | tf_op jit(solution)/shard_map/ppermute | solution.py:19
  (59 other events, 658.5 us)
Sparse Core Ops, SparseCore 0:
  10.3 66.6 all-gather.3
  78.7 41.3 all-gather.5
  182.8 36.7 reduce-scatter.4
  227.3 66.9 reduce-scatter.2
